TPU v7x, 32 devices: a whole 2x2x4 slice. The times are simulated.
32 devices in a mesh: tok: 8 (over z, core), feat: 4 (over y, x).
Axes of the slice: x: 2, y: 2, z: 4, core: 2. Of those that a mesh axis runs over, the one named last changes fastest.
Arguments:
- teacher: float32 [4096, 16384], P('tok', 'feat'), may hold values from -720 to 720, as said below
- student: float32 [4096, 2048], P('tok', 'feat'), may hold values from -6 to 6
- gain: float32 [16384], P('feat'), may hold values from 0.1 to 1.9
- projector: float32 [2048, 16384], P(None, 'feat'), may hold values from -0.1875 to 0.1875
- momentum: float32 [2048, 16384], P('tok', 'feat'), may hold values from -0.12 to 0.12
Outputs:
- new_projector: float32 [2048, 16384], P('tok', 'feat')
- new_momentum: float32 [2048, 16384], P('tok', 'feat')
- student_grad: float32 [4096, 2048], P('tok', 'feat')
- loss_value: float32 [], replicated
Inputs may be any that keep to these rules, and one draw needn't show every extreme that they name: `teacher`: finite real values.
All inputs are finite; a program needn't handle non-finite values.
Results may differ from a plain program's by a relative error of at most 0.00011.
Values sent between devices are 32-bit elements; how exact they have to be, the bound alone decides.
A program may use at most 192 MiB of HBM per device.

v0:
```python
import jax
import jax.numpy as jnp
from jax import lax
from jax.sharding import PartitionSpec as P

DT = 16384


norm_eps = 1e-05
momentum_rate = 0.9
step_rate = 0.5


def on_device(teacher, student, gain, projector, momentum):
    highest = lax.Precision.HIGHEST
    local_rows = teacher.shape[0]
    token_count = local_rows * lax.axis_size("tok")
    full_student = lax.all_gather(student, "feat", axis=1, tiled=True)
    predicted = jnp.dot(
        full_student, projector, precision=highest, preferred_element_type=jnp.float32
    )
    weighted = teacher * gain[None, :]
    squares_part = jnp.sum(teacher * teacher, axis=1)
    row_total = lax.psum(squares_part, "feat")
    row_scale = lax.rsqrt(row_total / DT + norm_eps)
    residual = predicted - weighted * row_scale[:, None]
    error_sum = lax.psum(jnp.sum(residual * residual), ("tok", "feat"))
    loss_value = error_sum / (token_count * DT)
    own_count = projector.shape[0] // lax.axis_size("tok")
    grad_terms = (
        lax.dot_general(
            full_student,
            residual,
            (((0,), (0,)), ((), ())),
            precision=highest,
            preferred_element_type=jnp.float32,
        )
        / token_count
    )
    proj_grad = lax.psum_scatter(grad_terms, "tok", scatter_dimension=0, tiled=True)
    student_terms = lax.dot_general(
        residual,
        projector,
        (((1,), (1,)), ((), ())),
        precision=highest,
        preferred_element_type=jnp.float32,
    )
    student_grad = lax.psum_scatter(student_terms, "feat", scatter_dimension=1, tiled=True)
    new_momentum = momentum_rate * momentum + proj_grad
    first_own = lax.axis_index("tok") * own_count
    own_rows = lax.dynamic_slice_in_dim(projector, first_own, own_count, 0)
    new_projector = own_rows - step_rate * new_momentum
    return (new_projector, new_momentum, student_grad, loss_value)


def solution(mesh):
    in_specs = (P("tok", "feat"), P("tok", "feat"), P("feat"), P(None, "feat"), P("tok", "feat"))
    out_specs = (P("tok", "feat"), P("tok", "feat"), P("tok", "feat"), P())
    return jax.shard_map(
        on_device, mesh=mesh, in_specs=in_specs, out_specs=out_specs, check_vma=False
    )
```

profile of v0, /device:TPU:0, one launch (start us, length us, event | category | flops | bytes accessed | tf_op | source)
XLA Modules:
  0.0 577.5 jit_solution(7482827443139206293)
XLA Ops:
  7.2 0.0 copy-start.2
  7.2 0.0 all-gather.2.cloned.1.call-start
  7.2 0.7 all-gather.2.cloned.1.call-update
  7.9 0.0 reduce-scatter.3.cloned.1.call-start
  8.0 4.0 multiply_reduce_fusion
  12.0 11.4 %psum.14 = f32[512]{0:T(512)S(1)} all-reduce(f32[512]{0:T(512)S(1)} %multiply_reduce_fusion), channel_id=1, replica_groups=mesh['tok'=8,'feat'=4] {'feat'}, use_global_device_ids=true, to_apply=%region_1.0 | all-reduce | flops 512 | bytes 4096 | tf_op jit(solution)/shard_map/psum | solution.py:24
  23.3 42.0 %all-gather.2.cloned.1.call-done = f32[512,2048]{1,0:T(8,128)} async-done(((f32[512,512]{1,0:T(8,128)}), f32[512,2048]{1,0:T(8,128)}) %all-gather.2.cloned.1.call-update) | async-done | bytes 4194320 | tf_op jit(solution)/shard_map/all_gather | solution.py:18
  65.3 0.0 copy-done.2
  65.3 0.0 copy-start.1
  65.3 60.9 %fusion.6 = (f32[]{:T(128)}, f32[512,4096]{1,0:T(8,128)S(1)}) fusion(f32[512,4096]{1,0:T(8,128)} %param.5, f32[512]{0:T(512)S(1)} %add_rsqrt_fusion, f32[4096]{0:T(1024)S(1)} %copy-done.2, f32[512,2048]{1,0:T(8,128)} %all-gather.2.cloned.1.call-done, f32[2048,4096]{1,0:T(8,128)} %param.8), kind=kOutput, calls=%fused_computation.6 | convolution fusion | flops 51550093312 | bytes 54544388 | tf_op jit(solution)/shard_map/dot_general | solution.py:19
  126.2 0.0 copy-start
  126.2 3.2 copy-done
  129.4 0.0 copy-done.1
  129.4 58.9 %multiply_bitcast_fusion = f32[2048,4096]{0,1:T(8,128)} fusion(f32[512,2048]{1,0:T(8,128)S(1)} %copy-done.1, f32[512,4096]{1,0:T(8,128)S(1)} %get-tuple-element.11, f32[512,4096]{1,0:T(8,128)} %param.5, f32[512]{0:T(512)S(1)} %add_rsqrt_fusion, f32[4096]{0:T(1024)S(1)} %copy-done.2), kind=kOutput, calls=%fused_computation | convolution fusion | flops 51554287616 | bytes 54544384 | tf_op jit(solution)/shard_map/dot_general | solution.py:31
  188.2 0.0 reduce-scatter.3.cloned.1.call-update
  188.3 0.0 reduce-scatter.5.cloned.1.call-start
  188.3 61.2 %fusion = f32[512,2048]{1,0:T(8,128)} fusion(f32[2048,4096]{1,0:T(8,128)} %param.8, f32[512,4096]{1,0:T(8,128)} %copy-done, f32[512,4096]{1,0:T(8,128)} %param.5, f32[512]{0:T(512)S(1)} %add_rsqrt_fusion, f32[4096]{0:T(1024)S(1)} %copy-done.2), kind=kOutput, calls=%fused_computation.2 | convolution fusion | flops 51545899008 | bytes 54544384 | tf_op jit(solution)/shard_map/dot_general | solution.py:41
  249.5 0.0 reduce-scatter.5.cloned.1.call-update
  249.6 4.7 constant_dynamic-slice_fusion
  254.3 5.6 copy.13
  259.9 5.6 copy.10
  265.5 41.1 %psum.15 = f32[]{:T(128)} all-reduce(f32[]{:T(128)} %get-tuple-element.10), channel_id=1, replica_groups=mesh['tok'=8,'feat'=4] {'tok','feat'}, use_global_device_ids=true, to_apply=%region_5.0 | all-reduce | flops 1 | bytes 8 | tf_op jit(solution)/shard_map/psum | solution.py:27
  307.2 207.8 %reduce-scatter.3.cloned.1.call-done = f32[256,4096]{0,1:T(8,128)} async-done(((f32[2048,4096]{0,1:T(8,128)}), f32[256,4096]{0,1:T(8,128)}) %reduce-scatter.3.cloned.1.call-update) | async-done | bytes 4194320 | tf_op jit(solution)/shard_map/reduce_scatter | solution.py:40
  515.0 8.9 %multiply_subtract_fusion = (f32[256,4096]{0,1:T(8,128)}, f32[256,4096]{0,1:T(8,128)}) fusion(f32[256,4096]{0,1:T(8,128)} %copy.13, f32[256,4096]{0,1:T(8,128)} %reduce-scatter.3.cloned.1.call-done, f32[256,4096]{0,1:T(8,128)} %copy.10), kind=kLoop, calls=%fused_computation.9 | loop fusion | flops 4194304 | bytes 20971520 | tf_op jit(solution)/shard_map/sub | solution.py:52
  523.9 5.6 copy.11
  529.5 5.9 %copy.12 = f32[256,4096]{1,0:T(8,128)} copy(f32[256,4096]{0,1:T(8,128)} %get-tuple-element.9) | data formatting | bytes 8388608
  535.4 34.4 %reduce-scatter.5.cloned.1.call-done = f32[512,512]{1,0:T(8,128)} async-done(((f32[512,2048]{1,0:T(8,128)}), f32[512,512]{1,0:T(8,128)}) %reduce-scatter.5.cloned.1.call-update) | async-done | bytes 1048592 | tf_op jit(solution)/shard_map/reduce_scatter | solution.py:48
  (1 shorter events, 0.0 us)
Async XLA Ops:
  7.2 58.1 %copy-start.2 = (f32[4096]{0:T(1024)S(1)}, f32[4096]{0:T(1024)}, u32[]{:S(2)}) copy-start(f32[4096]{0:T(1024)} %param.7) | copy-start | bytes 49156
  7.2 58.1 %all-gather.2.cloned.1.call-start = ((), (), s32[]{:S(2)}) async-start(), calls=%async_computation.2 | async-start | bytes 5242880 | tf_op jit(solution)/shard_map/all_gather | solution.py:18
  7.9 507.1 %reduce-scatter.3.cloned.1.call-start = ((), (), s32[]{:S(2)}) async-start(), calls=%async_computation.3 | async-start | bytes 37748736 | tf_op jit(solution)/shard_map/reduce_scatter | solution.py:40
  65.3 64.1 %copy-start.1 = (f32[512,2048]{1,0:T(8,128)S(1)}, f32[512,2048]{1,0:T(8,128)}, u32[]{:S(2)}) copy-start(f32[512,2048]{1,0:T(8,128)} %all-gather.2.cloned.1.call-done) | copy-start | bytes 12582916
  126.2 3.2 copy-start
  188.3 381.6 %reduce-scatter.5.cloned.1.call-start = ((), (), s32[]{:S(2)}) async-start(), calls=%async_computation.4 | async-start | bytes 5242880 | tf_op jit(solution)/shard_map/reduce_scatter | solution.py:48
Sparse Core Ops, SparseCore 0:
  9.9 55.3 all-gather.1
  188.4 326.5 reduce-scatter.2
  518.8 50.9 reduce-scatter.4
where the time goes:
time: 578 us
  waiting for transfers between devices  285 us (49%)
  matrix products  181 us (31%)
  blocking collectives  52.5 us (9%)
  local copies, waits for them, and re-layouts  30.7 us (5%)
  between operations  15.5 us (3%)
  other arithmetic  12.9 us (2%)
    reduce_scatter x1, waiting for transfers between devices, on_device(): lax.psum_scatter(grad_terms, 'tok', scatter_dimension=0, tiled=True)  208 us
    dot_general x1, matrix products, on_device(): lax.dot_general(residual, projector, (((1,), (1,)), ((), ())), precision=...  61.2 us
    dot_general x1, matrix products, on_device(): jnp.dot(full_student, projector, precision=highest, preferred_element_typ...  60.9 us
    dot_general x1, matrix products, on_device(): lax.dot_general(full_student, residual, (((0,), (0,)), ((), ())), precisi...  58.9 us
    all_gather x1, waiting for transfers between devices, on_device(): full_student = lax.all_gather(student, 'feat', axis=1, tiled=True)  42 us
    psum x1, blocking collectives, on_device(): error_sum = lax.psum(jnp.sum(residual * residual), ('tok', 'feat'))  41.1 us
    reduce_scatter x1, waiting for transfers between devices, on_device(): lax.psum_scatter(student_terms, 'feat', scatter_dimension=1, tiled=True)  34.4 us
    unnamed x10, local copies, waits for them, and re-layouts  26 us
  transfers between devices with their start and end apart: 3, of which 3 were waited for; matrix products, arithmetic and copies ran while one was open for 18% of the time, Pallas kernels for 0%

commit v1 on v0

v1 whole, which is shorter than its diff:
```python
import jax
import jax.numpy as jnp
from jax import lax
from jax.sharding import PartitionSpec as P

norm_eps = 1e-05
momentum_rate = 0.9
step_rate = 0.5
PIECES = 4


def product(a, b, ca, cb):
    return lax.dot_general(
        a,
        b,
        (((ca,), (cb,)), ((), ())),
        precision=lax.Precision.HIGH,
        preferred_element_type=jnp.float32,
    )


def on_device(teacher, student, gain, projector, momentum):
    rows, cols = teacher.shape
    tok = lax.axis_size("tok")
    feat = lax.axis_size("feat")
    chips = tok // 2
    own = momentum.shape[0]
    me = lax.axis_index("tok")
    chip, core = me // 2, me % 2
    token_count = rows * tok
    width = cols // PIECES
    swap = [(i, i ^ 1) for i in range(tok)]

    full_student = lax.all_gather(student, "feat", axis=1, tiled=True)
    squares = jnp.sum(teacher * teacher, axis=1)
    row_total = lax.psum(squares, "feat")
    row_scale = lax.rsqrt(row_total / (cols * feat) + norm_eps)[:, None]

    def columns_of(index):
        blocks = [
            lax.dynamic_slice_in_dim(full_student, (2 * i + index) * own, own, 1)
            for i in range(chips)
        ]
        return jnp.concatenate(blocks, axis=1)

    mine = columns_of(core)
    other = lax.ppermute(columns_of(1 - core), "tok", swap)

    def pick(terms, index):
        return lax.dynamic_index_in_dim(terms, index, 0, False)

    tie = lax.optimization_barrier
    residuals, swaps, firsts, all_terms, got, done = [], [], [], [], {}, []

    def predict(p, after):
        part = slice(p * width, (p + 1) * width)
        states = tie((full_student, after))[0]
        predicted = product(states, projector[:, part], 1, 0)
        residual = predicted - teacher[:, part] * row_scale * gain[None, part]
        residuals.append(residual)
        swaps.append(lax.ppermute(residual, "tok", swap))

    def own_terms(p, after):
        states = tie((mine, residuals[p], after))
        firsts.append(product(states[0], states[1], 0, 0))

    def other_terms(p, after):
        states = tie((other, swaps[p], after))
        terms = firsts[p] + product(states[0], states[1], 0, 0)
        all_terms.append(tie(terms).reshape(chips, own, width))

    def exchange(p, s):
        ups = [(2 * i + c, 2 * i + 2 + c) for i in range(s + 1) for c in range(2)]
        downs = [(tok - 1 - a, tok - 1 - b) for a, b in ups]
        send = (
            pick(all_terms[p], jnp.minimum(chips - 1 - s + chip, chips - 1)),
            pick(all_terms[p], jnp.maximum(s - (chips - 1) + chip, 0)),
        )
        if s:
            send = (send[0] + got[p][0], send[1] + got[p][1])
        send = tie((send, done[-2:-1]))[0]
        moved = lax.ppermute(send[0], "tok", ups), lax.ppermute(send[1], "tok", downs)
        got[p] = tie(moved)
        done.append(got[p])

    share = projector.shape[0] // PIECES
    student_parts = []

    def student_part(p, after):
        residual = jnp.concatenate(residuals, axis=1)
        held = tie((residual, after))[0]
        block = projector[p * share : (p + 1) * share]
        student_parts.append(product(held, block, 1, 1))

    steps = []
    for p in range(PIECES):
        steps += [(predict, p), (own_terms, p), (other_terms, p)]
    ahead, steps = steps[:6], steps[6:] + [(student_part, p) for p in range(PIECES)]
    after = row_scale
    for step, p in ahead:
        step(p, after)
    order = []
    for p in range(0, PIECES, 2):
        order += [(q, s) for s in range(chips - 1) for q in (p, p + 1)]
    for k, (p, s) in enumerate(order):
        exchange(p, s)
        if k >= 1 and steps:
            step, q = steps.pop(0)
            step(q, done[k - 1])
        if k == len(order) - 2:
            squares_of = [tie((r, done[k - 1]))[0] for r in residuals]
            error_sum = sum(jnp.sum(r * r) for r in squares_of)
            error_total = lax.psum(error_sum, ("tok", "feat"))
    student_terms = jnp.concatenate(student_parts, axis=1)
    student_grad = lax.psum_scatter(student_terms, "feat", scatter_dimension=1, tiled=True)
    loss_value = error_total / (token_count * cols * feat)
    totals = [pick(all_terms[p], chip) + got[p][0] + got[p][1] for p in range(PIECES)]

    proj_grad = jnp.concatenate(totals, axis=1) / token_count
    new_momentum = momentum_rate * momentum + proj_grad
    own_rows = lax.dynamic_slice_in_dim(projector, me * own, own, 0)
    new_projector = own_rows - step_rate * new_momentum
    return (new_projector, new_momentum, student_grad, loss_value)


def solution(mesh):
    in_specs = (P("tok", "feat"), P("tok", "feat"), P("feat"), P(None, "feat"), P("tok", "feat"))
    out_specs = (P("tok", "feat"), P("tok", "feat"), P("tok", "feat"), P())
    return jax.shard_map(
        on_device, mesh=mesh, in_specs=in_specs, out_specs=out_specs, check_vma=False
    )
```

time: 578 us -> 492 us (0.85); the launches traced: 578 us -> 484 us
  waiting for transfers between devices: 285 us -> 145 us
  starting transfers between devices: 0.12 us -> 80.2 us
  matrix products: 181 us -> 126 us
  other arithmetic: 12.9 us -> 49.4 us
  local copies, waits for them, and re-layouts: 30.7 us -> 10.5 us
    reduce_scatter x1 -> x0, waiting for transfers between devices: 208 us -> none  [on_device(): lax.psum_scatter(grad_terms, 'tok', scatter_dimension=0, tiled=True)]
    ppermute x0 -> x29, waiting for transfers between devices: none -> 103 us  [the longest x12 103 us: exchange(): lax.ppermute(send[0], 'tok', ups)]
    ppermute x0 -> x29, starting transfers between devices: none -> 80.1 us  [the longest x12 66.2 us: exchange(): lax.ppermute(send[0], 'tok', ups)]
    dot_general x3 -> x16, matrix products: 181 us -> 126 us  [product(): lax.dot_general(a, b, (((ca,), (cb,)), ((), ())), precision=lax.Precision...]
    reduce_scatter x1, waiting for transfers between devices: 34.4 us -> 0.01 us  [on_device(): lax.psum_scatter(student_terms, 'feat', scatter_dimension=1, tiled=True)]
    add x0 -> x12, other arithmetic: none -> 22 us  [the longest x8 13.5 us: exchange(): send = (send[0] + got[p][0], send[1] + got[p][1])]
    unnamed x10 -> x49, local copies, waits for them, and re-layouts: 26 us -> 6.69 us
    reduce_sum x1 -> x5, other arithmetic: 4.01 us -> 13.5 us  [the longest x4 9.5 us: on_device(): error_sum = sum((jnp.sum(r * r) for r in squares_of))]
  transfers between devices with their start and end apart: 3 -> 31, of which waited for: 3 -> 10; matrix products, arithmetic and copies ran while one was open for 18% -> 28% of each run, Pallas kernels for 0% -> 0%
where the time goes in v1:
time: 492 us; the launch traced here: 484 us
  waiting for transfers between devices  145 us (29%)
  matrix products  126 us (26%)
  starting transfers between devices  80.2 us (16%)
  blocking collectives  53.5 us (11%)
  other arithmetic  49.4 us (10%)
  between operations  19.5 us (4%)
  local copies, waits for them, and re-layouts  10.5 us (2%)
    dot_general x16, matrix products, product(): lax.dot_general(a, b, (((ca,), (cb,)), ((), ())), precision=lax.Precision...  126 us
    ppermute x12, waiting for transfers between devices, exchange(): lax.ppermute(send[0], 'tok', ups)  103 us
    ppermute x12, starting transfers between devices, exchange(): lax.ppermute(send[0], 'tok', ups)  66.2 us
    psum x1, blocking collectives, on_device(): error_total = lax.psum(error_sum, ('tok', 'feat'))  42.1 us
    all_gather x1, waiting for transfers between devices, on_device(): full_student = lax.all_gather(student, 'feat', axis=1, tiled=True)  41.9 us
    add x8, other arithmetic, exchange(): send = (send[0] + got[p][0], send[1] + got[p][1])  13.5 us
    ppermute x12, starting transfers between devices, exchange(): lax.ppermute(send[1], 'tok', downs)  13.2 us
    psum x1, blocking collectives, on_device(): row_total = lax.psum(squares, 'feat')  11.4 us
  transfers between devices with their start and end apart: 31, of which 10 were waited for; matrix products, arithmetic and copies ran while one was open for 28% of the time, Pallas kernels for 0%

profile of v1, /device:TPU:0, one launch (start us, length us, event | category | flops | bytes accessed | tf_op | source)
XLA Modules:
  0.0 484.4 jit_solution(14298824858918202327)
XLA Ops:
  12.0 11.4 %psum.14 = f32[512]{0:T(512)S(1)} all-reduce(f32[512]{0:T(512)S(1)} %multiply_reduce_fusion), channel_id=1, replica_groups=mesh['tok'=8,'feat'=4] {'feat'}, use_global_device_ids=true, to_apply=%region_1.2 | all-reduce | flops 512 | bytes 4096 | tf_op jit(solution)/shard_map/psum | solution.py:36
  23.4 41.9 %all-gather.2.cloned.1.call-done = f32[512,2048]{1,0:T(8,128)} async-done(((f32[512,512]{1,0:T(8,128)}), f32[512,2048]{1,0:T(8,128)}) %all-gather.2.cloned.1.call-update) | async-done | bytes 4194320 | tf_op jit(solution)/shard_map/all_gather | solution.py:34
  65.3 13.1 %multiply_subtract_fusion.3 = f32[512,1024]{1,0:T(8,128)} fusion(f32[512,4096]{1,0:T(8,128)} %param.5, f32[512,2048]{1,0:T(8,128)} %all-gather.2.cloned.1.call-done, f32[2048,4096]{1,0:T(8,128)} %param.8, f32[1024]{0:T(1024)S(1)} %get-tuple-element.197, f32[512]{0:T(512)S(1)} %add_rsqrt_fusion), kind=kOutput, calls=%fused_computation.34 | convolution fusion | flops 6444023808 | bytes 16783360 | tf_op jit(solution)/shard_map/dot_general | solution.py:13
  82.0 10.9 %multiply_subtract_fusion.4 = f32[512,1024]{1,0:T(8,128)} fusion(f32[512,4096]{1,0:T(8,128)} %param.5, f32[512,2048]{1,0:T(8,128)S(1)} %copy-done.11, f32[2048,4096]{1,0:T(8,128)} %param.8, f32[1024]{0:T(1024)S(1)} %get-tuple-element.198, f32[512]{0:T(512)S(1)} %add_rsqrt_fusion), kind=kOutput, calls=%fused_computation.35 | convolution fusion | flops 6444023808 | bytes 16783360 | tf_op jit(solution)/shard_map/dot_general | solution.py:13
  94.5 5.1 %fusion.31 = f32[1024,1024]{1,0:T(8,128)S(1)} fusion(f32[512,1024]{1,0:T(8,128)S(1)} %pad_maximum_fusion.2, f32[512,1024]{1,0:T(8,128)} %multiply_subtract_fusion.4), kind=kOutput, calls=%fused_computation.78 | convolution fusion | flops 3221225472 | bytes 8388608 | tf_op jit(solution)/shard_map/dot_general | solution.py:13
  99.6 5.1 %fusion.32 = f32[1024,1024]{1,0:T(8,128)S(1)} fusion(f32[512,1024]{1,0:T(8,128)S(1)} %pad_maximum_fusion.2, f32[512,1024]{1,0:T(8,128)} %multiply_subtract_fusion.3), kind=kOutput, calls=%fused_computation.79 | convolution fusion | flops 3221225472 | bytes 8388608 | tf_op jit(solution)/shard_map/dot_general | solution.py:13
  104.8 5.8 %convolution_add_fusion.3 = f32[1024,1024]{1,0:T(8,128)S(1)} fusion(f32[1024,1024]{1,0:T(8,128)S(1)} %fusion.31, f32[512,1024]{1,0:T(8,128)} %collective-permute-done, f32[512,1024]{1,0:T(8,128)} %collective-permute-done.1), kind=kOutput, calls=%fused_computation.25 | convolution fusion | flops 3222274048 | bytes 12582912 | tf_op jit(solution)/shard_map/dot_general | solution.py:13
  110.5 7.5 %convolution_add_fusion.2 = f32[1024,1024]{1,0:T(8,128)S(1)} fusion(f32[1024,1024]{1,0:T(8,128)S(1)} %fusion.32, f32[512,1024]{1,0:T(8,128)} %collective-permute-done, f32[512,1024]{1,0:T(8,128)} %collective-permute-done.8), kind=kOutput, calls=%fused_computation.24 | convolution fusion | flops 3222274048 | bytes 12582912 | tf_op jit(solution)/shard_map/dot_general | solution.py:13
  131.0 17.2 %collective-permute-done.2 = f32[256,1024]{1,0:T(8,128)} collective-permute-done((f32[256,1024]{1,0:T(8,128)}, f32[256,1024]{1,0:T(8,128)}, u32[]{:S(2)}, u32[]{:S(2)}) %collective-permute-start.2) | collective-permute-done | bytes 1048608 | tf_op jit(solution)/shard_map/ppermute | solution.py:82
  148.2 22.0 %collective-permute-done.9 = f32[256,1024]{1,0:T(8,128)} collective-permute-done((f32[256,1024]{1,0:T(8,128)}, f32[256,1024]{1,0:T(8,128)}, u32[]{:S(2)}, u32[]{:S(2)}) %collective-permute-start.9) | collective-permute-done | bytes 1048608 | tf_op jit(solution)/shard_map/ppermute | solution.py:82
  180.3 5.6 %collective-permute-start.4 = (f32[256,1024]{1,0:T(8,128)S(1)}, f32[256,1024]{1,0:T(8,128)S(1)}, u32[]{:S(2)}, u32[]{:S(2)}) collective-permute-start(f32[256,1024]{1,0:T(8,128)S(1)} %get-tuple-element.88), channel_id=1, source_target_pairs={{0,8},{4,12},{8,16},{12,20},{1,9},{5,13},{9,17},{13,21},{2,10},{6,... | collective-permute-start | bytes 3145736 | tf_op jit(solution)/shard_map/ppermute | solution.py:82
  186.7 10.4 %multiply_subtract_fusion.2 = f32[512,1024]{1,0:T(8,128)S(1)} fusion(f32[512,4096]{1,0:T(8,128)} %param.5, f32[512,2048]{1,0:T(8,128)S(1)} %copy-done.12, f32[2048,4096]{1,0:T(8,128)} %param.8, f32[1024]{0:T(1024)S(1)} %get-tuple-element.196, f32[512]{0:T(512)S(1)} %add_rsqrt_fusion), kind=kOutput, calls=%fused_computation.33 | convolution fusion | flops 6444023808 | bytes 16783360 | tf_op jit(solution)/shard_map/dot_general | solution.py:13
  202.6 9.5 %collective-permute-start.13 = (f32[256,1024]{1,0:T(8,128)S(1)}, f32[256,1024]{1,0:T(8,128)S(1)}, u32[]{:S(2)}, u32[]{:S(2)}) collective-permute-start(f32[256,1024]{1,0:T(8,128)S(1)} %get-tuple-element.108), channel_id=1, source_target_pairs={{0,8},{4,12},{8,16},{12,20},{16,24},{20,28},{1,9},{5,13},{9,17},{1... | collective-permute-start | bytes 3145736 | tf_op jit(solution)/shard_map/ppermute | solution.py:82
  213.3 10.2 %collective-permute-done.4 = f32[256,1024]{1,0:T(8,128)S(1)} collective-permute-done((f32[256,1024]{1,0:T(8,128)S(1)}, f32[256,1024]{1,0:T(8,128)S(1)}, u32[]{:S(2)}, u32[]{:S(2)}) %collective-permute-start.4) | collective-permute-done | bytes 1048608 | tf_op jit(solution)/shard_map/ppermute | solution.py:82
  225.3 9.5 %collective-permute-start.6 = (f32[256,1024]{1,0:T(8,128)}, f32[256,1024]{1,0:T(8,128)S(1)}, u32[]{:S(2)}, u32[]{:S(2)}) collective-permute-start(f32[256,1024]{1,0:T(8,128)} %get-tuple-element.92), channel_id=1, source_target_pairs={{0,8},{4,12},{8,16},{12,20},{16,24},{20,28},{1,9},{5,13},{9,17},{1... | collective-permute-start | bytes 3145736 | tf_op jit(solution)/shard_map/ppermute | solution.py:82
  236.1 10.7 %multiply_subtract_fusion.1 = f32[512,1024]{1,0:T(8,128)S(1)} fusion(f32[512,4096]{1,0:T(8,128)} %param.5, f32[512,2048]{1,0:T(8,128)S(1)} %copy-done.12, f32[2048,4096]{1,0:T(8,128)} %param.8, f32[1024]{0:T(1024)S(1)} %get-tuple-element.199, f32[512]{0:T(512)S(1)} %add_rsqrt_fusion), kind=kOutput, calls=%fused_computation.32 | convolution fusion | flops 6444023808 | bytes 16783360 | tf_op jit(solution)/shard_map/dot_general | solution.py:13
  254.4 12.9 %collective-permute-done.6 = f32[256,1024]{1,0:T(8,128)S(1)} collective-permute-done((f32[256,1024]{1,0:T(8,128)}, f32[256,1024]{1,0:T(8,128)S(1)}, u32[]{:S(2)}, u32[]{:S(2)}) %collective-permute-start.6) | collective-permute-done | bytes 1048608 | tf_op jit(solution)/shard_map/ppermute | solution.py:82
  267.3 6.1 %convolution_add_fusion.1 = f32[1024,1024]{1,0:T(8,128)S(1)} fusion(f32[1024,1024]{1,0:T(8,128)S(1)} %fusion.33, f32[512,1024]{1,0:T(8,128)} %collective-permute-done, f32[512,1024]{1,0:T(8,128)S(1)} %collective-permute-done.15), kind=kOutput, calls=%fused_computation.23 | convolution fusion | flops 3222274048 | bytes 12582912 | tf_op jit(solution)/shard_map/dot_general | solution.py:13
  273.7 8.7 %collective-permute-start.16 = (f32[256,1024]{1,0:T(8,128)S(1)}, f32[256,1024]{1,0:T(8,128)S(1)}, u32[]{:S(2)}, u32[]{:S(2)}) collective-permute-start(f32[256,1024]{1,0:T(8,128)S(1)} %get-tuple-element.117), channel_id=1, source_target_pairs={{0,8},{4,12},{1,9},{5,13},{2,10},{6,14},{3,11},{7,15}} | collective-permute-start | bytes 3145736 | tf_op jit(solution)/shard_map/ppermute | solution.py:82
  287.0 5.2 %convolution_add_fusion = f32[1024,1024]{1,0:T(8,128)S(1)} fusion(f32[1024,1024]{1,0:T(8,128)S(1)} %fusion.34, f32[512,1024]{1,0:T(8,128)} %collective-permute-done, f32[512,1024]{1,0:T(8,128)S(1)} %collective-permute-done.22), kind=kOutput, calls=%fused_computation.22 | convolution fusion | flops 3222274048 | bytes 12582912 | tf_op jit(solution)/shard_map/dot_general | solution.py:13
  294.6 11.3 %collective-permute-done.16 = f32[256,1024]{1,0:T(8,128)S(1)} collective-permute-done((f32[256,1024]{1,0:T(8,128)S(1)}, f32[256,1024]{1,0:T(8,128)S(1)}, u32[]{:S(2)}, u32[]{:S(2)}) %collective-permute-start.16) | collective-permute-done | bytes 1048608 | tf_op jit(solution)/shard_map/ppermute | solution.py:82
  311.5 9.3 %fusion.6 = f32[512,512]{0,1:T(8,128)S(1)} fusion(f32[512,4096]{1,0:T(8,128)S(1)} %pad_maximum_fusion, f32[2048,4096]{1,0:T(8,128)} %param.8), kind=kOutput, calls=%fused_computation.7 | convolution fusion | flops 6442450944 | bytes 17825792 | tf_op jit(solution)/shard_map/dot_general | solution.py:13
  320.8 7.5 %collective-permute-done.23 = f32[256,1024]{1,0:T(8,128)S(1)} collective-permute-done((f32[256,1024]{1,0:T(8,128)S(1)}, f32[256,1024]{1,0:T(8,128)S(1)}, u32[]{:S(2)}, u32[]{:S(2)}) %collective-permute-start.23) | collective-permute-done | bytes 1048608 | tf_op jit(solution)/shard_map/ppermute | solution.py:82
  334.2 9.3 %fusion.4 = f32[512,512]{0,1:T(8,128)S(1)} fusion(f32[512,4096]{1,0:T(8,128)S(1)} %pad_maximum_fusion, f32[2048,4096]{1,0:T(8,128)} %param.8), kind=kOutput, calls=%fused_computation.5 | convolution fusion | flops 6442450944 | bytes 17825792 | tf_op jit(solution)/shard_map/dot_general | solution.py:13
  343.5 7.3 %collective-permute-done.18 = f32[256,1024]{1,0:T(8,128)S(1)} collective-permute-done((f32[256,1024]{1,0:T(8,128)S(1)}, f32[256,1024]{1,0:T(8,128)S(1)}, u32[]{:S(2)}, u32[]{:S(2)}) %collective-permute-start.18) | collective-permute-done | bytes 1048608 | tf_op jit(solution)/shard_map/ppermute | solution.py:82
  350.9 9.7 %fusion.2 = f32[512,512]{0,1:T(8,128)S(1)} fusion(f32[512,4096]{1,0:T(8,128)S(1)} %pad_maximum_fusion, f32[2048,4096]{1,0:T(8,128)} %param.8), kind=kOutput, calls=%fused_computation.3 | convolution fusion | flops 6442450944 | bytes 17825792 | tf_op jit(solution)/shard_map/dot_general | solution.py:13
  360.6 10.2 %collective-permute-done.25 = f32[256,1024]{1,0:T(8,128)S(1)} collective-permute-done((f32[256,1024]{1,0:T(8,128)S(1)}, f32[256,1024]{1,0:T(8,128)S(1)}, u32[]{:S(2)}, u32[]{:S(2)}) %collective-permute-start.25) | collective-permute-done | bytes 1048608 | tf_op jit(solution)/shard_map/ppermute | solution.py:82
  370.8 10.3 %fusion = f32[512,512]{0,1:T(8,128)S(1)} fusion(f32[512,4096]{1,0:T(8,128)S(1)} %pad_maximum_fusion, f32[2048,4096]{1,0:T(8,128)} %param.8), kind=kOutput, calls=%fused_computation.1 | convolution fusion | flops 6442450944 | bytes 17825792 | tf_op jit(solution)/shard_map/dot_general | solution.py:13
  390.9 5.8 %collective-permute-start.20 = (f32[256,1024]{1,0:T(8,128)}, f32[256,1024]{1,0:T(8,128)}, u32[]{:S(2)}, u32[]{:S(2)}) collective-permute-start(f32[256,1024]{1,0:T(8,128)} %get-tuple-element.125), channel_id=1, source_target_pairs={{0,8},{4,12},{8,16},{12,20},{16,24},{20,28},{1,9},{5,13},{9,17},{1... | collective-permute-start | bytes 3145736 | tf_op jit(solution)/shard_map/ppermute | solution.py:82
  399.8 5.5 %collective-permute-start.27 = (f32[256,1024]{1,0:T(8,128)}, f32[256,1024]{1,0:T(8,128)}, u32[]{:S(2)}, u32[]{:S(2)}) collective-permute-start(f32[256,1024]{1,0:T(8,128)} %get-tuple-element.142), channel_id=1, source_target_pairs={{0,8},{4,12},{8,16},{12,20},{16,24},{20,28},{1,9},{5,13},{9,17},{1... | collective-permute-start | bytes 3145736 | tf_op jit(solution)/shard_map/ppermute | solution.py:82
  420.8 42.1 %psum.15 = f32[]{:T(128)} all-reduce(f32[]{:T(128)S(6)} %add.293), channel_id=1, replica_groups=mesh['tok'=8,'feat'=4] {'tok','feat'}, use_global_device_ids=true, to_apply=%region_7.8 | all-reduce | flops 1 | bytes 8 | tf_op jit(solution)/shard_map/psum | solution.py:113
  468.0 5.5 %multiply_subtract_fusion = (f32[256,4096]{1,0:T(8,128)}, f32[256,4096]{1,0:T(8,128)}) fusion(f32[2048,4096]{1,0:T(8,128)} %param.8, s32[]{:T(128)S(6)} %select_n.75, f32[256,1024]{1,0:T(8,128)S(1)} %fusion.25, f32[256,1024]{1,0:T(8,128)S(1)} %fusion.26, f32[256,1024]{1,0:T(8,128)S(1)} %fusion.27, f32[256,1024]{1,0:T(8,128)S(1)} %fusion.28, ...), kind=kLoop, calls=%fused_computation.21 | loop fusion | flops 8388608 | bytes 20971524 | tf_op jit(solution)/shard_map/sub | solution.py:122
  (127 shorter events, 102.2 us)
Async XLA Ops:
  7.2 58.1 %all-gather.2.cloned.1.call-start = ((), (), s32[]{:S(2)}) async-start(), calls=%async_computation.1 | async-start | bytes 5242880 | tf_op jit(solution)/shard_map/all_gather | solution.py:34
  7.9 465.6 %reduce-scatter.2.cloned.1.call-start = ((), (), s32[]{:S(2)}) async-start(), calls=%async_computation.2 | async-start | bytes 5242880 | tf_op jit(solution)/shard_map/reduce_scatter | solution.py:115
  78.4 26.3 %collective-permute-start.8 = (f32[512,1024]{1,0:T(8,128)}, f32[512,1024]{1,0:T(8,128)}, u32[]{:S(2)}, u32[]{:S(2)}) collective-permute-start(f32[512,1024]{1,0:T(8,128)} %multiply_subtract_fusion.3), channel_id=1, source_target_pairs={{0,4},{4,0},{8,12},{12,8},{16,20},{20,16},{24,28},{28,24},{1,5},{5... | collective-permute-start | bytes 6291464 | tf_op jit(solution)/shard_map/ppermute | solution.py:61
  81.5 23.2 %collective-permute-start = (f32[512,1024]{1,0:T(8,128)}, f32[512,1024]{1,0:T(8,128)}, u32[]{:S(2)}, u32[]{:S(2)}) collective-permute-start(f32[512,1024]{1,0:T(8,128)} %pad_maximum_fusion.3), channel_id=1, source_target_pairs={{0,4},{4,0},{8,12},{12,8},{16,20},{20,16},{24,28},{28,24},{1,5},{5... | collective-permute-start | bytes 6291464 | tf_op jit(solution)/shard_map/ppermute | solution.py:47
  92.9 11.9 %collective-permute-start.1 = (f32[512,1024]{1,0:T(8,128)}, f32[512,1024]{1,0:T(8,128)}, u32[]{:S(2)}, u32[]{:S(2)}) collective-permute-start(f32[512,1024]{1,0:T(8,128)} %multiply_subtract_fusion.4), channel_id=1, source_target_pairs={{0,4},{4,0},{8,12},{12,8},{16,20},{20,16},{24,28},{28,24},{1,5},{5... | collective-permute-start | bytes 6291464 | tf_op jit(solution)/shard_map/ppermute | solution.py:61
  121.0 27.2 %collective-permute-start.2 = (f32[256,1024]{1,0:T(8,128)}, f32[256,1024]{1,0:T(8,128)}, u32[]{:S(2)}, u32[]{:S(2)}) collective-permute-start(f32[256,1024]{1,0:T(8,128)} %get-tuple-element.84), channel_id=1, source_target_pairs={{0,8},{4,12},{1,9},{5,13},{2,10},{6,14},{3,11},{7,15}} | collective-permute-start | bytes 3145736 | tf_op jit(solution)/shard_map/ppermute | solution.py:82
  125.4 22.8 %collective-permute-start.3 = (f32[256,1024]{1,0:T(8,128)}, f32[256,1024]{1,0:T(8,128)}, u32[]{:S(2)}, u32[]{:S(2)}) collective-permute-start(f32[256,1024]{1,0:T(8,128)} %get-tuple-element.85), channel_id=1, source_target_pairs={{28,20},{24,16},{29,21},{25,17},{30,22},{26,18},{31,23},{27,19}} | collective-permute-start | bytes 3145736 | tf_op jit(solution)/shard_map/ppermute | solution.py:82
  127.0 43.2 %collective-permute-start.9 = (f32[256,1024]{1,0:T(8,128)}, f32[256,1024]{1,0:T(8,128)}, u32[]{:S(2)}, u32[]{:S(2)}) collective-permute-start(f32[256,1024]{1,0:T(8,128)} %get-tuple-element.100), channel_id=1, source_target_pairs={{0,8},{4,12},{1,9},{5,13},{2,10},{6,14},{3,11},{7,15}} | collective-permute-start | bytes 3145736 | tf_op jit(solution)/shard_map/ppermute | solution.py:82
  129.3 40.9 %collective-permute-start.10 = (f32[256,1024]{1,0:T(8,128)S(1)}, f32[256,1024]{1,0:T(8,128)}, u32[]{:S(2)}, u32[]{:S(2)}) collective-permute-start(f32[256,1024]{1,0:T(8,128)S(1)} %get-tuple-element.101), channel_id=1, source_target_pairs={{28,20},{24,16},{29,21},{25,17},{30,22},{26,18},{31,23},{27,19}} | collective-permute-start | bytes 3145736 | tf_op jit(solution)/shard_map/ppermute | solution.py:82
  172.9 28.2 %collective-permute-start.11 = (f32[256,1024]{1,0:T(8,128)S(1)}, f32[256,1024]{1,0:T(8,128)S(1)}, u32[]{:S(2)}, u32[]{:S(2)}) collective-permute-start(f32[256,1024]{1,0:T(8,128)S(1)} %get-tuple-element.104), channel_id=1, source_target_pairs={{0,8},{4,12},{8,16},{12,20},{1,9},{5,13},{9,17},{13,21},{2,10},{6,... | collective-permute-start | bytes 3145736 | tf_op jit(solution)/shard_map/ppermute | solution.py:82
  177.6 23.5 %collective-permute-start.12 = (f32[256,1024]{1,0:T(8,128)S(1)}, f32[256,1024]{1,0:T(8,128)S(1)}, u32[]{:S(2)}, u32[]{:S(2)}) collective-permute-start(f32[256,1024]{1,0:T(8,128)S(1)} %get-tuple-element.105), channel_id=1, source_target_pairs={{28,20},{24,16},{20,12},{16,8},{29,21},{25,17},{21,13},{17,9},{30,... | collective-permute-start | bytes 3145736 | tf_op jit(solution)/shard_map/ppermute | solution.py:82
  180.3 43.2 %collective-permute-start.4 = (f32[256,1024]{1,0:T(8,128)S(1)}, f32[256,1024]{1,0:T(8,128)S(1)}, u32[]{:S(2)}, u32[]{:S(2)}) collective-permute-start(f32[256,1024]{1,0:T(8,128)S(1)} %get-tuple-element.88), channel_id=1, source_target_pairs={{0,8},{4,12},{8,16},{12,20},{1,9},{5,13},{9,17},{13,21},{2,10},{6,... | collective-permute-start | bytes 3145736 | tf_op jit(solution)/shard_map/ppermute | solution.py:82
  185.9 37.6 %collective-permute-start.5 = (f32[256,1024]{1,0:T(8,128)S(1)}, f32[256,1024]{1,0:T(8,128)S(1)}, u32[]{:S(2)}, u32[]{:S(2)}) collective-permute-start(f32[256,1024]{1,0:T(8,128)S(1)} %get-tuple-element.89), channel_id=1, source_target_pairs={{28,20},{24,16},{20,12},{16,8},{29,21},{25,17},{21,13},{17,9},{30,... | collective-permute-start | bytes 3145736 | tf_op jit(solution)/shard_map/ppermute | solution.py:82
  197.1 54.6 %copy-start.8 = (f32[512,1024]{1,0:T(8,128)}, f32[512,1024]{1,0:T(8,128)S(1)}, u32[]{:S(2)}) copy-start(f32[512,1024]{1,0:T(8,128)S(1)} %multiply_subtract_fusion.2) | copy-start | bytes 6291460
  197.1 70.2 %collective-permute-start.15 = (f32[512,1024]{1,0:T(8,128)S(1)}, f32[512,1024]{1,0:T(8,128)S(1)}, u32[]{:S(2)}, u32[]{:S(2)}) collective-permute-start(f32[512,1024]{1,0:T(8,128)S(1)} %multiply_subtract_fusion.2), channel_id=1, source_target_pairs={{0,4},{4,0},{8,12},{12,8},{16,20},{20,16},{24,28},{28,24},{1,5},{5... | collective-permute-start | bytes 6291464 | tf_op jit(solution)/shard_map/ppermute | solution.py:61
  202.6 44.2 %collective-permute-start.13 = (f32[256,1024]{1,0:T(8,128)S(1)}, f32[256,1024]{1,0:T(8,128)S(1)}, u32[]{:S(2)}, u32[]{:S(2)}) collective-permute-start(f32[256,1024]{1,0:T(8,128)S(1)} %get-tuple-element.108), channel_id=1, source_target_pairs={{0,8},{4,12},{8,16},{12,20},{16,24},{20,28},{1,9},{5,13},{9,17},{1... | collective-permute-start | bytes 3145736 | tf_op jit(solution)/shard_map/ppermute | solution.py:82
  212.0 42.3 %collective-permute-start.14 = (f32[256,1024]{1,0:T(8,128)}, f32[256,1024]{1,0:T(8,128)}, u32[]{:S(2)}, u32[]{:S(2)}) collective-permute-start(f32[256,1024]{1,0:T(8,128)} %get-tuple-element.109), channel_id=1, source_target_pairs={{28,20},{24,16},{20,12},{16,8},{12,4},{8,0},{29,21},{25,17},{21,13... | collective-permute-start | bytes 3145736 | tf_op jit(solution)/shard_map/ppermute | solution.py:82
  225.3 42.0 %collective-permute-start.6 = (f32[256,1024]{1,0:T(8,128)}, f32[256,1024]{1,0:T(8,128)S(1)}, u32[]{:S(2)}, u32[]{:S(2)}) collective-permute-start(f32[256,1024]{1,0:T(8,128)} %get-tuple-element.92), channel_id=1, source_target_pairs={{0,8},{4,12},{8,16},{12,20},{16,24},{20,28},{1,9},{5,13},{9,17},{1... | collective-permute-start | bytes 3145736 | tf_op jit(solution)/shard_map/ppermute | solution.py:82
  234.8 32.5 %collective-permute-start.7 = (f32[256,1024]{1,0:T(8,128)}, f32[256,1024]{1,0:T(8,128)S(1)}, u32[]{:S(2)}, u32[]{:S(2)}) collective-permute-start(f32[256,1024]{1,0:T(8,128)} %get-tuple-element.93), channel_id=1, source_target_pairs={{28,20},{24,16},{20,12},{16,8},{12,4},{8,0},{29,21},{25,17},{21,13... | collective-permute-start | bytes 3145736 | tf_op jit(solution)/shard_map/ppermute | solution.py:82
  247.8 39.2 %collective-permute-start.22 = (f32[512,1024]{1,0:T(8,128)S(1)}, f32[512,1024]{1,0:T(8,128)S(1)}, u32[]{:S(2)}, u32[]{:S(2)}) collective-permute-start(f32[512,1024]{1,0:T(8,128)S(1)} %multiply_subtract_fusion.1), channel_id=1, source_target_pairs={{0,4},{4,0},{8,12},{12,8},{16,20},{20,16},{24,28},{28,24},{1,5},{5... | collective-permute-start | bytes 6291464 | tf_op jit(solution)/shard_map/ppermute | solution.py:61
  273.7 32.2 %collective-permute-start.16 = (f32[256,1024]{1,0:T(8,128)S(1)}, f32[256,1024]{1,0:T(8,128)S(1)}, u32[]{:S(2)}, u32[]{:S(2)}) collective-permute-start(f32[256,1024]{1,0:T(8,128)S(1)} %get-tuple-element.117), channel_id=1, source_target_pairs={{0,8},{4,12},{1,9},{5,13},{2,10},{6,14},{3,11},{7,15}} | collective-permute-start | bytes 3145736 | tf_op jit(solution)/shard_map/ppermute | solution.py:82
  282.4 23.5 %collective-permute-start.17 = (f32[256,1024]{1,0:T(8,128)S(1)}, f32[256,1024]{1,0:T(8,128)S(1)}, u32[]{:S(2)}, u32[]{:S(2)}) collective-permute-start(f32[256,1024]{1,0:T(8,128)S(1)} %get-tuple-element.118), channel_id=1, source_target_pairs={{28,20},{24,16},{29,21},{25,17},{30,22},{26,18},{31,23},{27,19}} | collective-permute-start | bytes 3145736 | tf_op jit(solution)/shard_map/ppermute | solution.py:82
  292.5 35.9 %collective-permute-start.23 = (f32[256,1024]{1,0:T(8,128)S(1)}, f32[256,1024]{1,0:T(8,128)S(1)}, u32[]{:S(2)}, u32[]{:S(2)}) collective-permute-start(f32[256,1024]{1,0:T(8,128)S(1)} %get-tuple-element.134), channel_id=1, source_target_pairs={{0,8},{4,12},{1,9},{5,13},{2,10},{6,14},{3,11},{7,15}} | collective-permute-start | bytes 3145736 | tf_op jit(solution)/shard_map/ppermute | solution.py:82
  293.8 34.5 %collective-permute-start.24 = (f32[256,1024]{1,0:T(8,128)S(1)}, f32[256,1024]{1,0:T(8,128)S(1)}, u32[]{:S(2)}, u32[]{:S(2)}) collective-permute-start(f32[256,1024]{1,0:T(8,128)S(1)} %get-tuple-element.135), channel_id=1, source_target_pairs={{28,20},{24,16},{29,21},{25,17},{30,22},{26,18},{31,23},{27,19}} | collective-permute-start | bytes 3145736 | tf_op jit(solution)/shard_map/ppermute | solution.py:82
  306.3 44.5 %collective-permute-start.18 = (f32[256,1024]{1,0:T(8,128)S(1)}, f32[256,1024]{1,0:T(8,128)S(1)}, u32[]{:S(2)}, u32[]{:S(2)}) collective-permute-start(f32[256,1024]{1,0:T(8,128)S(1)} %get-tuple-element.121), channel_id=1, source_target_pairs={{0,8},{4,12},{8,16},{12,20},{1,9},{5,13},{9,17},{13,21},{2,10},{6,... | collective-permute-start | bytes 3145736 | tf_op jit(solution)/shard_map/ppermute | solution.py:82
  310.8 40.1 %collective-permute-start.19 = (f32[256,1024]{1,0:T(8,128)S(1)}, f32[256,1024]{1,0:T(8,128)S(1)}, u32[]{:S(2)}, u32[]{:S(2)}) collective-permute-start(f32[256,1024]{1,0:T(8,128)S(1)} %get-tuple-element.122), channel_id=1, source_target_pairs={{28,20},{24,16},{20,12},{16,8},{29,21},{25,17},{21,13},{17,9},{30,... | collective-permute-start | bytes 3145736 | tf_op jit(solution)/shard_map/ppermute | solution.py:82
  328.8 42.0 %collective-permute-start.25 = (f32[256,1024]{1,0:T(8,128)S(1)}, f32[256,1024]{1,0:T(8,128)S(1)}, u32[]{:S(2)}, u32[]{:S(2)}) collective-permute-start(f32[256,1024]{1,0:T(8,128)S(1)} %get-tuple-element.138), channel_id=1, source_target_pairs={{0,8},{4,12},{8,16},{12,20},{1,9},{5,13},{9,17},{13,21},{2,10},{6,... | collective-permute-start | bytes 3145736 | tf_op jit(solution)/shard_map/ppermute | solution.py:82
  333.2 37.5 %collective-permute-start.26 = (f32[256,1024]{1,0:T(8,128)S(1)}, f32[256,1024]{1,0:T(8,128)S(1)}, u32[]{:S(2)}, u32[]{:S(2)}) collective-permute-start(f32[256,1024]{1,0:T(8,128)S(1)} %get-tuple-element.139), channel_id=1, source_target_pairs={{28,20},{24,16},{20,12},{16,8},{29,21},{25,17},{21,13},{17,9},{30,... | collective-permute-start | bytes 3145736 | tf_op jit(solution)/shard_map/ppermute | solution.py:82
  390.9 72.0 %collective-permute-start.20 = (f32[256,1024]{1,0:T(8,128)}, f32[256,1024]{1,0:T(8,128)}, u32[]{:S(2)}, u32[]{:S(2)}) collective-permute-start(f32[256,1024]{1,0:T(8,128)} %get-tuple-element.125), channel_id=1, source_target_pairs={{0,8},{4,12},{8,16},{12,20},{16,24},{20,28},{1,9},{5,13},{9,17},{1... | collective-permute-start | bytes 3145736 | tf_op jit(solution)/shard_map/ppermute | solution.py:82
  396.7 66.2 %collective-permute-start.21 = (f32[256,1024]{1,0:T(8,128)}, f32[256,1024]{1,0:T(8,128)}, u32[]{:S(2)}, u32[]{:S(2)}) collective-permute-start(f32[256,1024]{1,0:T(8,128)} %get-tuple-element.126), channel_id=1, source_target_pairs={{28,20},{24,16},{20,12},{16,8},{12,4},{8,0},{29,21},{25,17},{21,13... | collective-permute-start | bytes 3145736 | tf_op jit(solution)/shard_map/ppermute | solution.py:82
  399.8 66.0 %collective-permute-start.27 = (f32[256,1024]{1,0:T(8,128)}, f32[256,1024]{1,0:T(8,128)}, u32[]{:S(2)}, u32[]{:S(2)}) collective-permute-start(f32[256,1024]{1,0:T(8,128)} %get-tuple-element.142), channel_id=1, source_target_pairs={{0,8},{4,12},{8,16},{12,20},{16,24},{20,28},{1,9},{5,13},{9,17},{1... | collective-permute-start | bytes 3145736 | tf_op jit(solution)/shard_map/ppermute | solution.py:82
  405.3 60.5 %collective-permute-start.28 = (f32[256,1024]{1,0:T(8,128)}, f32[256,1024]{1,0:T(8,128)}, u32[]{:S(2)}, u32[]{:S(2)}) collective-permute-start(f32[256,1024]{1,0:T(8,128)} %get-tuple-element.143), channel_id=1, source_target_pairs={{28,20},{24,16},{20,12},{16,8},{12,4},{8,0},{29,21},{25,17},{21,13... | collective-permute-start | bytes 3145736 | tf_op jit(solution)/shard_map/ppermute | solution.py:82
  (23 other events, 325.3 us)
Sparse Core Ops, SparseCore 0:
  9.8 55.3 all-gather.1
  383.9 52.3 reduce-scatter.1
